TPU v7x, 32 devices: a whole 2x2x4 slice. The times are simulated.
32 devices in a mesh: parts: 2 (over x), grp: 2 (over core), row: 8 (over z, y).
Axes of the slice: x: 2, y: 2, z: 4, core: 2. Of those that a mesh axis runs over, the one named last changes fastest.
Arguments:
- design: bfloat16 [8192, 1024], P(('parts', 'grp', 'row')), parts along dimension 0, may hold values from -6 to 6
- target: float32 [8192], P(('parts', 'grp', 'row')), parts along dimension 0, may hold values from -6 to 6
- coeffs: bfloat16 [2048], P('parts'), parts along dimension 0, may hold values from -0.1875 to 0.1875
- tau_level: int32 [64], P(('parts', 'grp', 'row')), parts along dimension 0, may hold values from 0 to 3
- bucket: int32 [8192], P(('parts', 'grp', 'row')), parts along dimension 0, may hold values from 0 to 63
- sign_bit: int32 [8192], P(('parts', 'grp', 'row')), parts along dimension 0, may hold values from 0 to 1
- panel_order: int32 [16], P('parts'), parts along dimension 0, may hold values from 0 to 7, each once
Outputs:
- rotated: float32 [2048, 1024], P(('parts', 'grp'), 'row'), parts along dimension 0
There are 2 independent parts, one for each index of `parts`. A program takes and returns all parts, laid end to end along the dimension named above; each array names one. Nothing has to cross between parts.
Inputs may be any that keep to these rules, and one draw needn't show every extreme that they name: `panel_order`: each of 0 to 7 once.
All inputs are finite; a program needn't handle non-finite values. Where the computation divides by a largest or mean magnitude, that divisor is 1e-20 or more.
Results may differ from a plain program's by a relative error of at most 0.0044.
Values may be sent and summed in bfloat16 or wider, within the bound.
A program may use at most 64 MiB of HBM per device.

v0:
```python
import functools

import jax
import jax.numpy as jnp
from jax import lax
from jax.experimental import pallas as pl
from jax.experimental.pallas import tpu as pltpu
from jax.sharding import PartitionSpec as P

PANEL = 128
KB = 64
ROUNDS = 5
NS_ITERS = 4
CHUNKS = 2
MESH = pl.DeviceIdType.MESH
F32 = jnp.float32
BF16 = jnp.bfloat16


def dot(left, right):
    return jnp.dot(left, right, preferred_element_type=F32)


def cross(left, right):
    return lax.dot_general(left, right, (((0,), (0,)), ((), ())), preferred_element_type=F32)


def split(value):
    high = value.astype(BF16)
    return high, (value - high.astype(F32)).astype(BF16)


def product(left, right):
    return dot(left[0], right[0]) + (dot(left[0], right[1]) + dot(left[1], right[0]))


def stacked(upper, lower):
    return tuple(jnp.concatenate(pair, axis=0) for pair in zip(upper, lower))


def transform_columns(gram, width):
    size = gram.shape[0]
    same = lax.broadcasted_iota(jnp.int32, gram.shape, 0) == lax.broadcasted_iota(
        jnp.int32, gram.shape, 1
    )
    diagonal = jnp.where(same, gram, 0.0)
    squares_row = jnp.sum(diagonal, axis=0, keepdims=True)
    squares_col = jnp.sum(diagonal, axis=1, keepdims=True)
    inv_row = lax.rsqrt(squares_row)
    inv_col = lax.rsqrt(squares_col)
    normed = gram * inv_col * inv_row
    bound = jnp.max(jnp.sum(jnp.abs(normed), axis=0, keepdims=True), axis=1, keepdims=True)
    current = normed / bound

    def middle_of(value):
        return jnp.where(same, 1.5, 0.0) - 0.5 * value

    middle = split(middle_of(current))
    inverse = middle
    current = split(product(split(current), middle))
    for iteration in range(1, NS_ITERS):
        middle = split(middle_of(product(inverse, current)))
        if iteration < NS_ITERS - 1:
            both = product(stacked(current, inverse), middle)
            current = split(both[:size])
            inverse = split(both[size:])
    inverse = product(middle, tuple(part[:, :width] for part in inverse))
    return inv_col * inverse * (jnp.sqrt(squares_row[:, :width]) / jnp.sqrt(bound))


def kernel(
    count,
    design_ref, target_ref, coeffs_ref, tau_ref, bucket_ref, sign_ref, order_ref,
    out_ref,
    piece, own, owned, partner, mine_self, mine_other, their_self, their_other,
    deal_send, deal_recv, pass_send, pass_recv, swap_send, swap_recv, gram_send, gram_recv,
):
    me = lax.axis_index("row")
    sibling = {"grp": 1 - lax.axis_index("grp")}
    depth = count.bit_length() - 1
    half = count * KB
    chunk = half // CHUNKS

    def paired(turn):
        step = 1 << (turn % depth)
        return {"row": me + step * (1 - 2 * ((me // step) % 2))}

    def remote(source, target, send, recv, device):
        return pltpu.make_async_remote_copy(
            src_ref=source, dst_ref=target, send_sem=send, recv_sem=recv,
            device_id=device, device_id_type=MESH,
        )

    barrier = pltpu.get_barrier_semaphore()
    for away in range(1, count):
        pl.semaphore_signal(
            barrier, inc=1, device_id={"row": lax.rem(me + away, count)}, device_id_type=MESH
        )
    pl.semaphore_signal(barrier, inc=1, device_id=sibling, device_id_type=MESH)

    rows = design_ref.shape[0]
    fitted = lax.dot_general(
        jnp.broadcast_to(coeffs_ref[...], (16, coeffs_ref.shape[1])),
        design_ref[...],
        (((1,), (1,)), ((), ())),
        preferred_element_type=F32,
    )[:1]
    residual = target_ref[...] - fitted
    blocks = tau_ref.shape[0]
    lane = lax.broadcasted_iota(jnp.int32, (1, rows), 1)
    level = jnp.zeros((1, rows), F32)
    for block in range(blocks):
        first = block * (rows // blocks)
        level = jnp.where(lane >= first, tau_ref[block].astype(F32), level)
    quantile = 0.1 + 0.25 * level
    upper = jax.nn.sigmoid(residual / 0.2)
    weight = (quantile * upper + (1.0 - quantile) * (1.0 - upper)) / jnp.sqrt(
        residual * residual + 0.25
    )
    signed = (2.0 * sign_ref[...].astype(F32) - 1.0) * jnp.sqrt(weight)
    slots = lax.broadcasted_iota(jnp.int32, (KB, rows), 0)
    embed = jnp.where(slots == bucket_ref[...], signed, 0.0).astype(BF16)

    sketch = dot(embed, design_ref[...])

    def sketch_of(position):
        wanted = jnp.full((KB, PANEL), order_ref[position], jnp.int32)
        chosen = sketch[:, :PANEL]
        for panel in range(1, count):
            chosen = jnp.where(
                wanted == panel, sketch[:, panel * PANEL : (panel + 1) * PANEL], chosen
            )
        return chosen.astype(BF16)

    def rows_of(source):
        return pl.ds(pl.multiple_of(source * KB, KB), KB)

    pl.semaphore_wait(barrier, count)

    def deal(away, position):
        return remote(
            piece.at[away], owned.at[0, rows_of(me)], deal_send.at[away], deal_recv.at[me],
            {"row": position},
        )

    for away in range(1, count):
        position = lax.rem(me + away, count)
        piece[away] = sketch_of(position)
        deal(away, position).start()
    owned[0, rows_of(me), :] = sketch_of(me)

    def passed(source):
        return remote(
            owned.at[0, rows_of(source)], partner.at[0, rows_of(source)],
            pass_send.at[source], pass_recv.at[source], paired(0),
        )

    passed(me).start()
    for away in range(1, count):
        source = lax.rem(me + count - away, count)
        remote(
            piece.at[away], owned.at[0, rows_of(source)], deal_send.at[away],
            deal_recv.at[source], {"row": source},
        ).wait_recv()
        passed(source).start()

    def swap(turn, index):
        part = pl.ds(index * chunk, chunk)
        return remote(
            owned.at[turn, part], partner.at[turn, part],
            swap_send.at[turn, index], swap_recv.at[turn, index], paired(turn),
        )

    def self_copy(turn):
        return remote(
            mine_self.at[turn], their_self.at[turn], gram_send.at[turn, 0],
            gram_recv.at[turn, 0], sibling,
        )

    def other_copy(turn):
        return remote(
            mine_other.at[turn], their_other.at[turn], gram_send.at[turn, 1],
            gram_recv.at[turn, 1], sibling,
        )

    for turn in range(ROUNDS):
        held = owned[turn]
        mine_self[turn] = cross(held, held)
        self_copy(turn).start()
        if turn == 0:
            for source in range(count):
                passed(source).wait_recv()
        else:
            for index in range(CHUNKS):
                swap(turn, index).wait_recv()
        both = jnp.concatenate([held, partner[turn]], axis=1)
        mine_other[turn] = cross(partner[turn], both)
        other_copy(turn).start()
        self_copy(turn).wait_recv()
        self_gram = mine_self[turn] + their_self[turn]
        other_copy(turn).wait_recv()
        other_gram = mine_other[turn] + their_other[turn]
        gram = jnp.concatenate(
            [
                jnp.concatenate([self_gram, other_gram[:, :PANEL].T], axis=1),
                other_gram,
            ],
            axis=0,
        )
        high, low = split(transform_columns(gram, PANEL))
        mixing = jnp.concatenate([high, low], axis=1)
        for index in range(CHUNKS):
            part = pl.ds(index * chunk, chunk)
            bulk = dot(
                jnp.concatenate([owned[turn, part, :], partner[turn, part, :]], axis=1), mixing
            )
            fresh = bulk[:, :PANEL] + bulk[:, PANEL:]
            if turn > 0:
                rest = (own[part, :] - owned[turn, part, :].astype(F32)).astype(BF16)
                fresh = fresh + dot(rest, high[:PANEL])
            if turn < ROUNDS - 1:
                own[part, :] = fresh
                owned[turn + 1, part, :] = fresh.astype(BF16)
                swap(turn + 1, index).start()
            else:
                out_ref[part, :] = fresh

    for away in range(1, count):
        deal(away, lax.rem(me + away, count)).wait_send()
    for source in range(count):
        passed(source).wait_send()
    for turn in range(ROUNDS):
        self_copy(turn).wait_send()
        other_copy(turn).wait_send()
        if turn > 0:
            for index in range(CHUNKS):
                swap(turn, index).wait_send()


def per_device(count, design, target, coeffs, tau_level, bucket, sign_bit, panel_order):
    half = count * KB
    vmem = pl.BlockSpec(memory_space=pltpu.VMEM)
    smem = pl.BlockSpec(memory_space=pltpu.SMEM)
    dma = pltpu.SemaphoreType.DMA
    return pl.pallas_call(
        functools.partial(kernel, count),
        out_shape=jax.ShapeDtypeStruct((half, PANEL), F32),
        in_specs=[vmem, vmem, vmem, smem, vmem, vmem, smem],
        out_specs=vmem,
        scratch_shapes=[
            pltpu.VMEM((count, KB, PANEL), BF16),
            pltpu.VMEM((half, PANEL), F32),
            pltpu.VMEM((ROUNDS, half, PANEL), BF16),
            pltpu.VMEM((ROUNDS, half, PANEL), BF16),
            pltpu.VMEM((ROUNDS, PANEL, PANEL), F32),
            pltpu.VMEM((ROUNDS, PANEL, 2 * PANEL), F32),
            pltpu.VMEM((ROUNDS, PANEL, PANEL), F32),
            pltpu.VMEM((ROUNDS, PANEL, 2 * PANEL), F32),
            dma((count,)), dma((count,)), dma((count,)), dma((count,)),
            dma((ROUNDS, CHUNKS)), dma((ROUNDS, CHUNKS)), dma((ROUNDS, 2)), dma((ROUNDS, 2)),
        ],
        compiler_params=pltpu.CompilerParams(
            collective_id=0, has_side_effects=True, vmem_limit_bytes=48 * 2**20
        ),
    )(
        design, target.reshape(1, -1), coeffs.reshape(1, -1), tau_level,
        bucket.reshape(1, -1), sign_bit.reshape(1, -1), panel_order,
    )


def solution(mesh):
    placed = (
        P(("parts", "grp", "row"), None),
        P(("parts", "grp", "row")),
        P("parts"),
        P(("parts", "grp", "row")),
        P(("parts", "grp", "row")),
        P(("parts", "grp", "row")),
        P("parts"),
    )
    return jax.shard_map(
        functools.partial(per_device, mesh.shape["row"]),
        mesh=mesh,
        in_specs=placed,
        out_specs=P(("parts", "grp"), "row"),
        check_vma=False,
    )
```

profile of v0, /device:TPU:9, one launch (start us, length us, event | category | flops | bytes accessed | tf_op | source)
XLA Modules:
  0.0 59.2 jit_solution(15332102386755050794)
XLA Ops:
  0.0 0.0 copy-start.6
  0.0 0.7 %copy-done.6 = bf16[1024]{0:T(1024)(128)(2,1)S(1)} copy-done((bf16[1024]{0:T(1024)(128)(2,1)S(1)}, bf16[1024]{0:T(1024)(128)(2,1)}, u32[]{:S(2)}) %copy-start.6) | copy-done | bytes 2072
  0.7 0.0 copy-start.1
  0.7 0.0 copy-start.2
  0.7 0.0 copy-start.3
  0.7 0.0 copy-start.4
  0.7 0.0 copy-start.5
  0.7 0.6 %copy-done.1 = f32[256]{0:T(256)S(1)} copy-done((f32[256]{0:T(256)S(1)}, f32[256]{0:T(256)}, u32[]{:S(2)}) %copy-start.1) | copy-done | bytes 1048
  1.4 0.0 copy-done.2
  1.4 0.0 copy-done.3
  1.4 0.0 copy-done.4
  1.4 0.0 copy-done.5
  1.4 0.0 copy-start
  1.4 1.0 %copy-done = bf16[256,1024]{1,0:T(8,128)(2,1)S(1)} copy-done((bf16[256,1024]{1,0:T(8,128)(2,1)S(1)}, bf16[256,1024]{1,0:T(8,128)(2,1)}, u32[]{:S(2)}) %copy-start) | copy-done | bytes 524312
  2.4 56.0 %shard_map.73 = f32[512,128]{1,0:T(8,128)S(1)} custom-call(bf16[256,1024]{1,0:T(8,128)(2,1)S(1)} %copy-done, f32[1,256]{1,0:T(1,128)S(1)} %bitcast.3, bf16[1,1024]{1,0:T(2,128)(2,1)S(1)} %reshape.13.coeffs_ref, s32[2]{0:T(128)S(1)} %copy-done.4, s32[1,256]{1,0:T(1,128)S(1)} %bitcast.4, s32[1,256]{1,0:T(1,128)S(1)} %bitcast.5, s32[8]{0:T(128)S(1)} %copy-done.5), custom_call_target="tpu_custom_call" | custom-call | tf_op jit(solution)/shard_map/pallas_call | solution.py:245
  58.5 0.7 %copy.9 = f32[512,128]{1,0:T(8,128)} copy(f32[512,128]{1,0:T(8,128)S(1)} %shard_map.73) | data formatting | bytes 524288
  (1 shorter events, 0.0 us)
Async XLA Ops:
  0.0 0.7 %copy-start.6 = (bf16[1024]{0:T(1024)(128)(2,1)S(1)}, bf16[1024]{0:T(1024)(128)(2,1)}, u32[]{:S(2)}) copy-start(bf16[1024]{0:T(1024)(128)(2,1)} %param.9) | copy-start | bytes 6148
  0.7 0.7 %copy-start.1 = (f32[256]{0:T(256)S(1)}, f32[256]{0:T(256)}, u32[]{:S(2)}) copy-start(f32[256]{0:T(256)} %param.8) | copy-start | bytes 3076
  0.7 0.7 %copy-start.2 = (s32[256]{0:T(256)S(1)}, s32[256]{0:T(256)}, u32[]{:S(2)}) copy-start(s32[256]{0:T(256)} %param.11) | copy-start | bytes 3076
  0.7 0.7 %copy-start.3 = (s32[256]{0:T(256)S(1)}, s32[256]{0:T(256)}, u32[]{:S(2)}) copy-start(s32[256]{0:T(256)} %param.12) | copy-start | bytes 3076
  0.7 0.7 %copy-start.4 = (s32[2]{0:T(128)S(1)}, s32[2]{0:T(128)}, u32[]{:S(2)}) copy-start(s32[2]{0:T(128)} %tau_ref.1) | copy-start | bytes 28
  0.7 0.7 %copy-start.5 = (s32[8]{0:T(128)S(1)}, s32[8]{0:T(128)}, u32[]{:S(2)}) copy-start(s32[8]{0:T(128)} %order_ref.1) | copy-start | bytes 100
  1.4 1.0 %copy-start = (bf16[256,1024]{1,0:T(8,128)(2,1)S(1)}, bf16[256,1024]{1,0:T(8,128)(2,1)}, u32[]{:S(2)}) copy-start(bf16[256,1024]{1,0:T(8,128)(2,1)} %design_ref.1) | copy-start | bytes 1572868
where the time goes:
time: 59.4 us; the launch traced here: 59.2 us
  Pallas kernels  56 us (94%)
  local copies, waits for them, and re-layouts  3.12 us (5%)
    pallas_call x1, Pallas kernels, per_device(): pl.pallas_call(functools.partial(kernel, count), out_shape=jax.ShapeDtype...  56 us
    unnamed x15, local copies, waits for them, and re-layouts  3.12 us

commit v1 on v0

--- a/solution.py
+++ b/solution.py
@@ -25,17 +25,20 @@
     return lax.dot_general(left, right, (((0,), (0,)), ((), ())), preferred_element_type=F32)
 
 
-def split(value):
-    high = value.astype(BF16)
-    return high, (value - high.astype(F32)).astype(BF16)
+def shifted(scale, rest):
+    return scale, rest, rest.astype(BF16)
+
+
+def mixed(left, right, square):
+    return shifted(left[0] * right[0], right[0] * left[1] + left[0] * right[1] + square)
 
 
 def product(left, right):
-    return dot(left[0], right[0]) + (dot(left[0], right[1]) + dot(left[1], right[0]))
-
-
-def stacked(upper, lower):
-    return tuple(jnp.concatenate(pair, axis=0) for pair in zip(upper, lower))
+    return mixed(left, right, dot(left[2], right[2]))
+
+
+def middle_of(value):
+    return shifted(1.5 - 0.5 * value[0], -0.5 * value[1])
 
 
 def transform_columns(gram, width):
@@ -50,22 +53,23 @@
     inv_col = lax.rsqrt(squares_col)
     normed = gram * inv_col * inv_row
     bound = jnp.max(jnp.sum(jnp.abs(normed), axis=0, keepdims=True), axis=1, keepdims=True)
-    current = normed / bound
-
-    def middle_of(value):
-        return jnp.where(same, 1.5, 0.0) - 0.5 * value
-
-    middle = split(middle_of(current))
+    share = 1.0 / bound
+    current = shifted(share, normed * share - jnp.where(same, share, 0.0))
+    middle = middle_of(current)
     inverse = middle
-    current = split(product(split(current), middle))
+    current = product(current, middle)
     for iteration in range(1, NS_ITERS):
-        middle = split(middle_of(product(inverse, current)))
+        middle = middle_of(product(inverse, current))
         if iteration < NS_ITERS - 1:
-            both = product(stacked(current, inverse), middle)
-            current = split(both[:size])
-            inverse = split(both[size:])
-    inverse = product(middle, tuple(part[:, :width] for part in inverse))
-    return inv_col * inverse * (jnp.sqrt(squares_row[:, :width]) / jnp.sqrt(bound))
+            squares = dot(jnp.concatenate([current[2], inverse[2]], axis=0), middle[2])
+            current = mixed(current, middle, squares[:size])
+            inverse = mixed(inverse, middle, squares[size:])
+    inverse = tuple([inverse[0]] + [part[:, :width] for part in inverse[1:]])
+    square = dot(middle[2], inverse[2])
+    scale, rest, _ = mixed((middle[0], middle[1][:, :width]), inverse, square)
+    root = lax.rsqrt(bound)
+    columns = inv_col * rest * (jnp.sqrt(squares_row[:, :width]) * root)
+    return scale * root, columns.astype(BF16)
 
 
 def kernel(
@@ -91,12 +95,18 @@
             device_id=device, device_id_type=MESH,
         )
 
+    parity = me % 2
+    groups = count // 2
+    group = me // 2
+
+    def place(number):
+        return 2 * number + parity
+
+    peers = [{"row": place(lax.rem(group + away, groups))} for away in range(1, groups)]
+    peers += [paired(0), sibling]
     barrier = pltpu.get_barrier_semaphore()
-    for away in range(1, count):
-        pl.semaphore_signal(
-            barrier, inc=1, device_id={"row": lax.rem(me + away, count)}, device_id_type=MESH
-        )
-    pl.semaphore_signal(barrier, inc=1, device_id=sibling, device_id_type=MESH)
+    for peer in peers:
+        pl.semaphore_signal(barrier, inc=1, device_id=peer, device_id_type=MESH)
 
     rows = design_ref.shape[0]
     fitted = lax.dot_general(
@@ -126,7 +136,7 @@
     def sketch_of(position):
         wanted = jnp.full((KB, PANEL), order_ref[position], jnp.int32)
         chosen = sketch[:, :PANEL]
-        for panel in range(1, count):
+        for panel in range(1, sketch.shape[1] // PANEL):
             chosen = jnp.where(
                 wanted == panel, sketch[:, panel * PANEL : (panel + 1) * PANEL], chosen
             )
@@ -135,34 +145,44 @@
     def rows_of(source):
         return pl.ds(pl.multiple_of(source * KB, KB), KB)
 
-    pl.semaphore_wait(barrier, count)
-
-    def deal(away, position):
-        return remote(
-            piece.at[away], owned.at[0, rows_of(me)], deal_send.at[away], deal_recv.at[me],
-            {"row": position},
-        )
-
-    for away in range(1, count):
-        position = lax.rem(me + away, count)
-        piece[away] = sketch_of(position)
-        deal(away, position).start()
-    owned[0, rows_of(me), :] = sketch_of(me)
-
-    def passed(source):
-        return remote(
-            owned.at[0, rows_of(source)], partner.at[0, rows_of(source)],
-            pass_send.at[source], pass_recv.at[source], paired(0),
-        )
-
-    passed(me).start()
-    for away in range(1, count):
-        source = lax.rem(me + count - away, count)
-        remote(
-            piece.at[away], owned.at[0, rows_of(source)], deal_send.at[away],
-            deal_recv.at[source], {"row": source},
-        ).wait_recv()
-        passed(source).start()
+    pl.semaphore_wait(barrier, len(peers))
+
+    first = (owned, partner)
+
+    def deal(away, side, source, device):
+        return remote(
+            piece.at[away, side], first[side].at[0, rows_of(source)],
+            deal_send.at[away, side], deal_recv.at[source // 2, side], device,
+        )
+
+    for away in range(1, groups):
+        position = place(lax.rem(group + away, groups))
+        for side in range(2):
+            piece[away, side] = sketch_of(position + side * (1 - 2 * parity))
+            deal(away, side, me, {"row": position}).start()
+    for side in range(2):
+        first[side][0, rows_of(me), :] = sketch_of(me + side * (1 - 2 * parity))
+
+    def passed(source, side):
+        return remote(
+            first[side].at[0, rows_of(source)], first[1 - side].at[0, rows_of(source)],
+            pass_send.at[source // 2, side], pass_recv.at[source // 2, side], paired(0),
+        )
+
+    def arrived(number, side):
+        source = 2 * number + 1 - parity
+        return remote(
+            first[1 - side].at[0, rows_of(source)], first[side].at[0, rows_of(source)],
+            pass_send.at[number, 1 - side], pass_recv.at[number, 1 - side], paired(0),
+        )
+
+    for side in range(2):
+        passed(me, side).start()
+    for away in range(1, groups):
+        source = place(lax.rem(group + groups - away, groups))
+        for side in range(2):
+            deal(away, side, source, {"row": source}).wait_recv()
+            passed(source, side).start()
 
     def swap(turn, index):
         part = pl.ds(index * chunk, chunk)
@@ -184,15 +204,21 @@
         )
 
     for turn in range(ROUNDS):
-        held = owned[turn]
-        mine_self[turn] = cross(held, held)
-        self_copy(turn).start()
+        if turn > 0:
+            held = owned[turn]
+            mine_self[turn] = cross(held, held)
+            self_copy(turn).start()
         if turn == 0:
-            for source in range(count):
-                passed(source).wait_recv()
+            for number in range(groups):
+                for side in range(2):
+                    arrived(number, side).wait_recv()
         else:
             for index in range(CHUNKS):
                 swap(turn, index).wait_recv()
+        if turn == 0:
+            held = owned[turn]
+            mine_self[turn] = cross(held, held)
+            self_copy(turn).start()
         both = jnp.concatenate([held, partner[turn]], axis=1)
         mine_other[turn] = cross(partner[turn], both)
         other_copy(turn).start()
@@ -207,17 +233,14 @@
             ],
             axis=0,
         )
-        high, low = split(transform_columns(gram, PANEL))
-        mixing = jnp.concatenate([high, low], axis=1)
+        scale, mixing = transform_columns(gram, PANEL)
         for index in range(CHUNKS):
             part = pl.ds(index * chunk, chunk)
-            bulk = dot(
-                jnp.concatenate([owned[turn, part, :], partner[turn, part, :]], axis=1), mixing
+            mine = owned[turn, part, :]
+            kept = own[part, :] if turn > 0 else mine.astype(F32)
+            fresh = scale * kept + dot(
+                jnp.concatenate([mine, partner[turn, part, :]], axis=1), mixing
             )
-            fresh = bulk[:, :PANEL] + bulk[:, PANEL:]
-            if turn > 0:
-                rest = (own[part, :] - owned[turn, part, :].astype(F32)).astype(BF16)
-                fresh = fresh + dot(rest, high[:PANEL])
             if turn < ROUNDS - 1:
                 own[part, :] = fresh
                 owned[turn + 1, part, :] = fresh.astype(BF16)
@@ -225,10 +248,11 @@
             else:
                 out_ref[part, :] = fresh
 
-    for away in range(1, count):
-        deal(away, lax.rem(me + away, count)).wait_send()
-    for source in range(count):
-        passed(source).wait_send()
+    for side in range(2):
+        for away in range(1, groups):
+            deal(away, side, me, {"row": place(lax.rem(group + away, groups))}).wait_send()
+        for number in range(groups):
+            passed(place(number), side).wait_send()
     for turn in range(ROUNDS):
         self_copy(turn).wait_send()
         other_copy(turn).wait_send()
@@ -248,7 +272,7 @@
         in_specs=[vmem, vmem, vmem, smem, vmem, vmem, smem],
         out_specs=vmem,
         scratch_shapes=[
-            pltpu.VMEM((count, KB, PANEL), BF16),
+            pltpu.VMEM((count // 2, 2, KB, PANEL), BF16),
             pltpu.VMEM((half, PANEL), F32),
             pltpu.VMEM((ROUNDS, half, PANEL), BF16),
             pltpu.VMEM((ROUNDS, half, PANEL), BF16),
@@ -256,7 +280,7 @@
             pltpu.VMEM((ROUNDS, PANEL, 2 * PANEL), F32),
             pltpu.VMEM((ROUNDS, PANEL, PANEL), F32),
             pltpu.VMEM((ROUNDS, PANEL, 2 * PANEL), F32),
-            dma((count,)), dma((count,)), dma((count,)), dma((count,)),
+            *[dma((count // 2, 2))] * 4,
             dma((ROUNDS, CHUNKS)), dma((ROUNDS, CHUNKS)), dma((ROUNDS, 2)), dma((ROUNDS, 2)),
         ],
         compiler_params=pltpu.CompilerParams(

time: 59.4 us -> 52.7 us (0.89)
  Pallas kernels: 56 us -> 49.3 us
    pallas_call x1, Pallas kernels: 56 us -> 49.3 us  [per_device(): pl.pallas_call(functools.partial(kernel, count), out_shape=jax.ShapeDtype...]
where the time goes in v1:
time: 52.7 us; the launch traced here: 52.5 us
  Pallas kernels  49.3 us (94%)
  local copies, waits for them, and re-layouts  3.12 us (6%)
    pallas_call x1, Pallas kernels, per_device(): pl.pallas_call(functools.partial(kernel, count), out_shape=jax.ShapeDtype...  49.3 us
    unnamed x15, local copies, waits for them, and re-layouts  3.12 us

profile of v1, /device:TPU:9, one launch (start us, length us, event | category | flops | bytes accessed | tf_op | source)
XLA Modules:
  0.0 52.5 jit_solution(1269198464796586175)
XLA Ops:
  0.0 0.0 copy-start.6
  0.0 0.7 %copy-done.6 = bf16[1024]{0:T(1024)(128)(2,1)S(1)} copy-done((bf16[1024]{0:T(1024)(128)(2,1)S(1)}, bf16[1024]{0:T(1024)(128)(2,1)}, u32[]{:S(2)}) %copy-start.6) | copy-done | bytes 2072
  0.7 0.0 copy-start.1
  0.7 0.0 copy-start.2
  0.7 0.0 copy-start.3
  0.7 0.0 copy-start.4
  0.7 0.0 copy-start.5
  0.7 0.6 %copy-done.1 = f32[256]{0:T(256)S(1)} copy-done((f32[256]{0:T(256)S(1)}, f32[256]{0:T(256)}, u32[]{:S(2)}) %copy-start.1) | copy-done | bytes 1048
  1.4 0.0 copy-done.2
  1.4 0.0 copy-done.3
  1.4 0.0 copy-done.4
  1.4 0.0 copy-done.5
  1.4 0.0 copy-start
  1.4 1.0 %copy-done = bf16[256,1024]{1,0:T(8,128)(2,1)S(1)} copy-done((bf16[256,1024]{1,0:T(8,128)(2,1)S(1)}, bf16[256,1024]{1,0:T(8,128)(2,1)}, u32[]{:S(2)}) %copy-start) | copy-done | bytes 524312
  2.4 49.3 %shard_map.73 = f32[512,128]{1,0:T(8,128)S(1)} custom-call(bf16[256,1024]{1,0:T(8,128)(2,1)S(1)} %copy-done, f32[1,256]{1,0:T(1,128)S(1)} %bitcast.3, bf16[1,1024]{1,0:T(2,128)(2,1)S(1)} %reshape.13.coeffs_ref, s32[2]{0:T(128)S(1)} %copy-done.4, s32[1,256]{1,0:T(1,128)S(1)} %bitcast.4, s32[1,256]{1,0:T(1,128)S(1)} %bitcast.5, s32[8]{0:T(128)S(1)} %copy-done.5), custom_call_target="tpu_custom_call" | custom-call | tf_op jit(solution)/shard_map/pallas_call | solution.py:269
  51.8 0.7 %copy.9 = f32[512,128]{1,0:T(8,128)} copy(f32[512,128]{1,0:T(8,128)S(1)} %shard_map.73) | data formatting | bytes 524288
  (1 shorter events, 0.0 us)
Async XLA Ops:
  0.0 0.7 %copy-start.6 = (bf16[1024]{0:T(1024)(128)(2,1)S(1)}, bf16[1024]{0:T(1024)(128)(2,1)}, u32[]{:S(2)}) copy-start(bf16[1024]{0:T(1024)(128)(2,1)} %param.9) | copy-start | bytes 6148
  0.7 0.7 %copy-start.1 = (f32[256]{0:T(256)S(1)}, f32[256]{0:T(256)}, u32[]{:S(2)}) copy-start(f32[256]{0:T(256)} %param.8) | copy-start | bytes 3076
  0.7 0.7 %copy-start.2 = (s32[256]{0:T(256)S(1)}, s32[256]{0:T(256)}, u32[]{:S(2)}) copy-start(s32[256]{0:T(256)} %param.11) | copy-start | bytes 3076
  0.7 0.7 %copy-start.3 = (s32[256]{0:T(256)S(1)}, s32[256]{0:T(256)}, u32[]{:S(2)}) copy-start(s32[256]{0:T(256)} %param.12) | copy-start | bytes 3076
  0.7 0.7 %copy-start.4 = (s32[2]{0:T(128)S(1)}, s32[2]{0:T(128)}, u32[]{:S(2)}) copy-start(s32[2]{0:T(128)} %tau_ref.1) | copy-start | bytes 28
  0.7 0.7 %copy-start.5 = (s32[8]{0:T(128)S(1)}, s32[8]{0:T(128)}, u32[]{:S(2)}) copy-start(s32[8]{0:T(128)} %order_ref.1) | copy-start | bytes 100
  1.4 1.0 %copy-start = (bf16[256,1024]{1,0:T(8,128)(2,1)S(1)}, bf16[256,1024]{1,0:T(8,128)(2,1)}, u32[]{:S(2)}) copy-start(bf16[256,1024]{1,0:T(8,128)(2,1)} %design_ref.1) | copy-start | bytes 1572868

commit v2 on v1

--- a/solution.py
+++ b/solution.py
@@ -76,7 +76,7 @@
     count,
     design_ref, target_ref, coeffs_ref, tau_ref, bucket_ref, sign_ref, order_ref,
     out_ref,
-    piece, own, owned, partner, mine_self, mine_other, their_self, their_other,
+    piece, own, owned, partner, mine_gram, their_gram,
     deal_send, deal_recv, pass_send, pass_recv, swap_send, swap_recv, gram_send, gram_recv,
 ):
     me = lax.axis_index("row")
@@ -191,23 +191,16 @@
             swap_send.at[turn, index], swap_recv.at[turn, index], paired(turn),
         )
 
-    def self_copy(turn):
-        return remote(
-            mine_self.at[turn], their_self.at[turn], gram_send.at[turn, 0],
-            gram_recv.at[turn, 0], sibling,
-        )
-
-    def other_copy(turn):
-        return remote(
-            mine_other.at[turn], their_other.at[turn], gram_send.at[turn, 1],
-            gram_recv.at[turn, 1], sibling,
+    def gram_copy(turn):
+        return remote(
+            mine_gram.at[turn], their_gram.at[turn], gram_send.at[turn],
+            gram_recv.at[turn], sibling,
         )
 
     for turn in range(ROUNDS):
         if turn > 0:
             held = owned[turn]
-            mine_self[turn] = cross(held, held)
-            self_copy(turn).start()
+            mine_gram[turn, :, 2 * PANEL :] = cross(held, held)
         if turn == 0:
             for number in range(groups):
                 for side in range(2):
@@ -217,18 +210,16 @@
                 swap(turn, index).wait_recv()
         if turn == 0:
             held = owned[turn]
-            mine_self[turn] = cross(held, held)
-            self_copy(turn).start()
+            mine_gram[turn, :, 2 * PANEL :] = cross(held, held)
         both = jnp.concatenate([held, partner[turn]], axis=1)
-        mine_other[turn] = cross(partner[turn], both)
-        other_copy(turn).start()
-        self_copy(turn).wait_recv()
-        self_gram = mine_self[turn] + their_self[turn]
-        other_copy(turn).wait_recv()
-        other_gram = mine_other[turn] + their_other[turn]
+        mine_gram[turn, :, : 2 * PANEL] = cross(partner[turn], both)
+        gram_copy(turn).start()
+        gram_copy(turn).wait_recv()
+        total = mine_gram[turn] + their_gram[turn]
+        other_gram = total[:, : 2 * PANEL]
         gram = jnp.concatenate(
             [
-                jnp.concatenate([self_gram, other_gram[:, :PANEL].T], axis=1),
+                jnp.concatenate([total[:, 2 * PANEL :], other_gram[:, :PANEL].T], axis=1),
                 other_gram,
             ],
             axis=0,
@@ -254,8 +245,7 @@
         for number in range(groups):
             passed(place(number), side).wait_send()
     for turn in range(ROUNDS):
-        self_copy(turn).wait_send()
-        other_copy(turn).wait_send()
+        gram_copy(turn).wait_send()
         if turn > 0:
             for index in range(CHUNKS):
                 swap(turn, index).wait_send()
@@ -276,12 +266,10 @@
             pltpu.VMEM((half, PANEL), F32),
             pltpu.VMEM((ROUNDS, half, PANEL), BF16),
             pltpu.VMEM((ROUNDS, half, PANEL), BF16),
-            pltpu.VMEM((ROUNDS, PANEL, PANEL), F32),
-            pltpu.VMEM((ROUNDS, PANEL, 2 * PANEL), F32),
-            pltpu.VMEM((ROUNDS, PANEL, PANEL), F32),
-            pltpu.VMEM((ROUNDS, PANEL, 2 * PANEL), F32),
+            pltpu.VMEM((ROUNDS, PANEL, 3 * PANEL), F32),
+            pltpu.VMEM((ROUNDS, PANEL, 3 * PANEL), F32),
             *[dma((count // 2, 2))] * 4,
-            dma((ROUNDS, CHUNKS)), dma((ROUNDS, CHUNKS)), dma((ROUNDS, 2)), dma((ROUNDS, 2)),
+            dma((ROUNDS, CHUNKS)), dma((ROUNDS, CHUNKS)), dma((ROUNDS,)), dma((ROUNDS,)),
         ],
         compiler_params=pltpu.CompilerParams(
             collective_id=0, has_side_effects=True, vmem_limit_bytes=48 * 2**20

time: 52.7 us -> 52.6 us (level)
  no operation moved by 1% of the time
where the time goes in v2:
time: 52.6 us; the launch traced here: 52.5 us
  Pallas kernels  49.3 us (94%)
  local copies, waits for them, and re-layouts  3.12 us (6%)
    pallas_call x1, Pallas kernels, per_device(): pl.pallas_call(functools.partial(kernel, count), out_shape=jax.ShapeDtype...  49.3 us
    unnamed x15, local copies, waits for them, and re-layouts  3.12 us

profile of v2, /device:TPU:9, one launch (start us, length us, event | category | flops | bytes accessed | tf_op | source)
XLA Modules:
  0.0 52.5 jit_solution(15124017819702245495)
XLA Ops:
  0.0 0.0 copy-start.6
  0.0 0.7 %copy-done.6 = bf16[1024]{0:T(1024)(128)(2,1)S(1)} copy-done((bf16[1024]{0:T(1024)(128)(2,1)S(1)}, bf16[1024]{0:T(1024)(128)(2,1)}, u32[]{:S(2)}) %copy-start.6) | copy-done | bytes 2072
  0.7 0.0 copy-start.1
  0.7 0.0 copy-start.2
  0.7 0.0 copy-start.3
  0.7 0.0 copy-start.4
  0.7 0.0 copy-start.5
  0.7 0.6 %copy-done.1 = f32[256]{0:T(256)S(1)} copy-done((f32[256]{0:T(256)S(1)}, f32[256]{0:T(256)}, u32[]{:S(2)}) %copy-start.1) | copy-done | bytes 1048
  1.4 0.0 copy-done.2
  1.4 0.0 copy-done.3
  1.4 0.0 copy-done.4
  1.4 0.0 copy-done.5
  1.4 0.0 copy-start
  1.4 1.0 %copy-done = bf16[256,1024]{1,0:T(8,128)(2,1)S(1)} copy-done((bf16[256,1024]{1,0:T(8,128)(2,1)S(1)}, bf16[256,1024]{1,0:T(8,128)(2,1)}, u32[]{:S(2)}) %copy-start) | copy-done | bytes 524312
  2.4 49.3 %shard_map.73 = f32[512,128]{1,0:T(8,128)S(1)} custom-call(bf16[256,1024]{1,0:T(8,128)(2,1)S(1)} %copy-done, f32[1,256]{1,0:T(1,128)S(1)} %bitcast.3, bf16[1,1024]{1,0:T(2,128)(2,1)S(1)} %reshape.13.coeffs_ref, s32[2]{0:T(128)S(1)} %copy-done.4, s32[1,256]{1,0:T(1,128)S(1)} %bitcast.4, s32[1,256]{1,0:T(1,128)S(1)} %bitcast.5, s32[8]{0:T(128)S(1)} %copy-done.5), custom_call_target="tpu_custom_call" | custom-call | tf_op jit(solution)/shard_map/pallas_call | solution.py:259
  51.7 0.7 %copy.9 = f32[512,128]{1,0:T(8,128)} copy(f32[512,128]{1,0:T(8,128)S(1)} %shard_map.73) | data formatting | bytes 524288
  (1 shorter events, 0.0 us)
Async XLA Ops:
  0.0 0.7 %copy-start.6 = (bf16[1024]{0:T(1024)(128)(2,1)S(1)}, bf16[1024]{0:T(1024)(128)(2,1)}, u32[]{:S(2)}) copy-start(bf16[1024]{0:T(1024)(128)(2,1)} %param.9) | copy-start | bytes 6148
  0.7 0.7 %copy-start.1 = (f32[256]{0:T(256)S(1)}, f32[256]{0:T(256)}, u32[]{:S(2)}) copy-start(f32[256]{0:T(256)} %param.8) | copy-start | bytes 3076
  0.7 0.7 %copy-start.2 = (s32[256]{0:T(256)S(1)}, s32[256]{0:T(256)}, u32[]{:S(2)}) copy-start(s32[256]{0:T(256)} %param.11) | copy-start | bytes 3076
  0.7 0.7 %copy-start.3 = (s32[256]{0:T(256)S(1)}, s32[256]{0:T(256)}, u32[]{:S(2)}) copy-start(s32[256]{0:T(256)} %param.12) | copy-start | bytes 3076
  0.7 0.7 %copy-start.4 = (s32[2]{0:T(128)S(1)}, s32[2]{0:T(128)}, u32[]{:S(2)}) copy-start(s32[2]{0:T(128)} %tau_ref.1) | copy-start | bytes 28
  0.7 0.7 %copy-start.5 = (s32[8]{0:T(128)S(1)}, s32[8]{0:T(128)}, u32[]{:S(2)}) copy-start(s32[8]{0:T(128)} %order_ref.1) | copy-start | bytes 100
  1.4 1.0 %copy-start = (bf16[256,1024]{1,0:T(8,128)(2,1)S(1)}, bf16[256,1024]{1,0:T(8,128)(2,1)}, u32[]{:S(2)}) copy-start(bf16[256,1024]{1,0:T(8,128)(2,1)} %design_ref.1) | copy-start | bytes 1572868
